TPU v7x, 32 devices: a whole 2x2x4 slice. The times are simulated.
32 devices in a mesh: grp: 2 (over y), seq: 4 (over z), mdl: 2 (over x), pair: 2 (over core).
Axes of the slice: x: 2, y: 2, z: 4, core: 2. Of those that a mesh axis runs over, the one named last changes fastest.
Arguments:
- resp_query: bfloat16 [8192, 8192], P(('grp', 'seq', 'pair'), 'mdl'), parts along dimension 0, may hold values from -6 to 6
- resp_key: bfloat16 [8192, 1024], P(('grp', 'seq', 'pair'), 'mdl'), parts along dimension 0, may hold values from -6 to 6
- response_value: bfloat16 [8192, 1024], P(('grp', 'seq', 'pair'), 'mdl'), parts along dimension 0, may hold values from -6 to 6
- readout: bfloat16 [8192, 8192], P(('grp', 'seq', 'pair'), 'mdl'), parts along dimension 0, may hold values from -0.0625 to 0.0625
- packed_prompt_key: bfloat16 [1024, 1024], P(('grp', 'seq', 'pair'), 'mdl'), parts along dimension 0, may hold values from -6 to 6
- packed_prompt_value: bfloat16 [1024, 1024], P(('grp', 'seq', 'pair'), 'mdl'), parts along dimension 0, may hold values from -6 to 6
- prompt_owner: int32 [1024], P('grp'), parts along dimension 0, may hold values from 0 to 3, never falling along the last dimension, each value on 1 to 256 neighbouring positions
- pair_slot: int32 [8], P(('grp', 'seq')), parts along dimension 0, may hold values from 0 to 3, each once
- domain_of: int32 [8], P(('grp', 'seq')), parts along dimension 0, may hold values from 0 to 7
- resp_blocks: int32 [16], P(('grp', 'seq', 'pair')), parts along dimension 0, may hold values from 1 to 4, 20 in all
- ref_logprob: float32 [16], P(('grp', 'seq', 'pair')), parts along dimension 0, may hold values from -8 to 8
Outputs:
- grad_query: bfloat16 [8192, 8192], P(('grp', 'seq', 'pair'), 'mdl'), parts along dimension 0
- grad_resp_key: bfloat16 [8192, 1024], P(('grp', 'seq', 'pair'), 'mdl'), parts along dimension 0
- grad_resp_value: bfloat16 [8192, 1024], P(('grp', 'seq', 'pair'), 'mdl'), parts along dimension 0
- grad_prompt_key: float32 [1024, 1024], P(('grp', 'seq', 'pair'), 'mdl'), parts along dimension 0
- grad_prompt_value: float32 [1024, 1024], P(('grp', 'seq', 'pair'), 'mdl'), parts along dimension 0
There are 2 independent parts, one for each index of `grp`. A program takes and returns all parts, laid end to end along the dimension named above; each array names one. Nothing has to cross between parts.
Inputs may be any that keep to these rules, and one draw needn't show every extreme that they name: `prompt_owner`: ids never fall along the prompt; every one of the 4 pairs owns at least one prompt token and the longest prompt has exactly 256 tokens. `pair_slot`: each pair is held at exactly one index. `resp_blocks`: some response fills all 4 blocks.
All inputs are finite; a program needn't handle non-finite values.
Results may differ from a plain program's by a relative error of at most 0.015.
Values may be sent and summed in bfloat16 or wider, within the bound.
A program may use at most 128 MiB of HBM per device.

v0:
```python
import jax
import jax.numpy as jnp
from jax import lax
from jax.sharding import PartitionSpec as P

HEAD_SIZE = 128
PROMPT_DEV = 64
BLK = 128
NDOM = 8


dpo_beta = 0.5
loss_scale = 256.0


def from_partner(value, axis, bit):
    mask = 2**bit
    pairs = [(source, source ^ mask) for source in range(lax.axis_size(axis))]
    return lax.ppermute(value, axis, pairs)


def product(form, left, right):
    return jnp.einsum(form, left, right, preferred_element_type=jnp.float32)


def by_head(value_arrays, key_value_heads):
    return jnp.moveaxis(
        value_arrays.reshape(value_arrays.shape[0], key_value_heads, -1, HEAD_SIZE), 1, 0
    )


def kv_by_head(value_arrays, key_value_heads):
    return jnp.moveaxis(
        value_arrays.reshape(value_arrays.shape[0], key_value_heads, HEAD_SIZE), 1, 0
    )


def merge_heads(value_arrays):
    return jnp.moveaxis(value_arrays, 0, 1).reshape(value_arrays.shape[1], -1)


def visibility(prompt_visible, row_count):
    order = jnp.arange(row_count)
    causal = order[None, :] <= order[:, None]
    prompt_wide = jnp.broadcast_to(prompt_visible[None, :], (row_count, prompt_visible.shape[0]))
    return (prompt_wide, causal)


def head_forward(queries, key_rows, value_rows, visible):
    scores = product("rgd,kd->grk", queries, key_rows) * queries.shape[-1] ** (-0.5)
    scores = jnp.where(visible[None], scores, -jnp.inf)
    row_max = jnp.max(scores, axis=-1, keepdims=True)
    exponent = jnp.exp(scores - row_max)
    row_sum = jnp.sum(exponent, axis=-1, keepdims=True)
    weights = (exponent / row_sum).astype(jnp.bfloat16)
    outputs = product("grk,kd->rgd", weights, value_rows)
    return (outputs, row_max + jnp.log(row_sum))


def head_backward(queries, key_rows, value_rows, visible, log_norm, grad_half, grad_row):
    scale_factor = queries.shape[-1] ** (-0.5)
    scores = product("rgd,kd->grk", queries, key_rows) * scale_factor
    weights = jnp.where(visible[None], jnp.exp(scores - log_norm), 0.0)
    grad_prob = product("rgd,kd->grk", grad_half, value_rows)
    grad_score = (weights * (grad_prob - grad_row)).astype(jnp.bfloat16)
    grad_value = product("grk,rgd->kd", weights.astype(jnp.bfloat16), grad_half)
    grad_query = product("grk,kd->rgd", grad_score, key_rows) * scale_factor
    grad_key = product("grk,rgd->kd", grad_score, queries) * scale_factor
    return (grad_query, grad_key, grad_value)


def sequence_forward(
    queries, resp_key, response_value, packed_prompt_key, packed_prompt_value, prompt_visible
):
    key_value_heads = resp_key.shape[1] // HEAD_SIZE
    prompt_wide, causal = visibility(prompt_visible, queries.shape[0])
    visible = jnp.concatenate([prompt_wide, causal], axis=1)
    key_all = kv_by_head(jnp.concatenate([packed_prompt_key, resp_key], axis=0), key_value_heads)
    value_all = kv_by_head(
        jnp.concatenate([packed_prompt_value, response_value], axis=0), key_value_heads
    )
    return lax.map(
        lambda operands: head_forward(operands[0], operands[1], operands[2], visible),
        (by_head(queries, key_value_heads), key_all, value_all),
    )


def per_device(
    resp_query,
    resp_key,
    response_value,
    readout,
    packed_prompt_key,
    packed_prompt_value,
    prompt_owner,
    pair_slot,
    domain_of,
    resp_blocks,
    ref_logprob,
):
    seq_count = lax.axis_size("seq")
    key_value_heads = resp_key.shape[1] // HEAD_SIZE
    row_count = resp_query.shape[0]
    width = packed_prompt_key.shape[1]
    gathered_key, gathered_value = (
        lax.all_gather(packed_prompt_key, ("seq", "pair"), axis=0, tiled=True),
        lax.all_gather(packed_prompt_value, ("seq", "pair"), axis=0, tiled=True),
    )
    total_rows = gathered_key.shape[0]
    window = 4 * PROMPT_DEV
    first_owned = jnp.sum(jnp.where(prompt_owner < pair_slot[0], 1, 0)).astype(jnp.int32)
    window_start = jnp.minimum(first_owned, total_rows - window)
    window_key = lax.dynamic_slice_in_dim(gathered_key, window_start, window, 0)
    window_value = lax.dynamic_slice_in_dim(gathered_value, window_start, window, 0)
    window_owner = lax.dynamic_slice_in_dim(prompt_owner, window_start, window, 0)
    prompt_visible = window_owner == pair_slot[0]
    outputs, log_norm = sequence_forward(
        resp_query, resp_key, response_value, window_key, window_value, prompt_visible
    )
    token_valid = jnp.arange(row_count) < resp_blocks[0] * BLK
    read_heads = by_head(readout, key_value_heads)
    partial_sum = jnp.sum(
        jnp.where(token_valid[None, :, None, None], outputs * read_heads.astype(jnp.float32), 0.0)
    )
    side = lax.axis_index("pair")
    domain_slots = jnp.arange(NDOM)
    counts = lax.psum(jnp.where(domain_slots == domain_of[0], 1.0, 0.0).astype(jnp.float32), "seq")
    own_gap = lax.psum(partial_sum, "mdl") - ref_logprob[0]
    other_gap = from_partner(own_gap, "pair", 0)
    chosen_gap = jnp.where(side == 0, own_gap, other_gap)
    rejected_gap = jnp.where(side == 0, other_gap, own_gap)
    margin = dpo_beta * (chosen_gap - rejected_gap)
    own_count = jnp.sum(jnp.where(domain_slots == domain_of[0], counts, 0.0))
    weight = seq_count / (NDOM * own_count)
    coef_chosen = -loss_scale * weight * dpo_beta * jax.nn.sigmoid(-margin)
    coef = jnp.where(side == 0, coef_chosen, -coef_chosen)
    grad_full = jnp.where(token_valid[:, None], coef * readout.astype(jnp.float32), 0.0)
    grad_heads = by_head(grad_full, key_value_heads)
    grad_row = jnp.moveaxis(jnp.sum(grad_heads * outputs, axis=-1), 1, 2)[..., None]
    grad_half = grad_heads.astype(jnp.bfloat16)
    query_heads = by_head(resp_query, key_value_heads)
    prompt_wide, causal = visibility(prompt_visible, row_count)

    def full_head(operands):
        query_prompt, key_prompt_h, value_prompt_h = head_backward(
            operands[0],
            operands[1],
            operands[2],
            prompt_wide,
            operands[5],
            operands[6],
            operands[7],
        )
        query_self, key_self_h, value_self_h = head_backward(
            operands[0], operands[3], operands[4], causal, operands[5], operands[6], operands[7]
        )
        return (query_prompt + query_self, key_prompt_h, value_prompt_h, key_self_h, value_self_h)

    results = lax.map(
        full_head,
        (
            query_heads,
            kv_by_head(window_key, key_value_heads),
            kv_by_head(window_value, key_value_heads),
            kv_by_head(resp_key, key_value_heads),
            kv_by_head(response_value, key_value_heads),
            log_norm,
            grad_half,
            grad_row,
        ),
    )
    query_grad = merge_heads(results[0])
    key_self = merge_heads(results[3])
    value_self = merge_heads(results[4])
    window_grads = jnp.concatenate([merge_heads(results[1]), merge_heads(results[2])], axis=1)
    placed = lax.dynamic_update_slice_in_dim(
        jnp.zeros((total_rows, 2 * width), jnp.float32), window_grads, window_start, 0
    )
    key_prompt, value_prompt = (
        lax.psum_scatter(
            placed[:, :width].astype(jnp.bfloat16), ("seq", "pair"), scatter_dimension=0, tiled=True
        ).astype(jnp.float32),
        lax.psum_scatter(
            placed[:, width:].astype(jnp.bfloat16), ("seq", "pair"), scatter_dimension=0, tiled=True
        ).astype(jnp.float32),
    )
    return (
        query_grad.astype(jnp.bfloat16),
        key_self.astype(jnp.bfloat16),
        value_self.astype(jnp.bfloat16),
        key_prompt,
        value_prompt,
    )


def solution(mesh):
    in_specs = (
        P(("grp", "seq", "pair"), "mdl"),
        P(("grp", "seq", "pair"), "mdl"),
        P(("grp", "seq", "pair"), "mdl"),
        P(("grp", "seq", "pair"), "mdl"),
        P(("grp", "seq", "pair"), "mdl"),
        P(("grp", "seq", "pair"), "mdl"),
        P("grp"),
        P(("grp", "seq")),
        P(("grp", "seq")),
        P(("grp", "seq", "pair")),
        P(("grp", "seq", "pair")),
    )
    out_specs = (
        P(("grp", "seq", "pair"), "mdl"),
        P(("grp", "seq", "pair"), "mdl"),
        P(("grp", "seq", "pair"), "mdl"),
        P(("grp", "seq", "pair"), "mdl"),
        P(("grp", "seq", "pair"), "mdl"),
    )
    return jax.shard_map(
        per_device, mesh=mesh, in_specs=in_specs, out_specs=out_specs, check_vma=False
    )
```

profile of v0, /device:TPU:0, one launch (start us, length us, event | category | flops | bytes accessed | tf_op | source)
XLA Modules:
  0.0 292.4 jit_solution(16925557524379775399)
XLA Ops:
  8.0 1.3 select_reduce_fusion.1
  10.0 16.8 %all_gather.6 = bf16[512,512]{1,0:T(8,128)(2,1)S(1)} all-gather(bf16[64,512]{1,0:T(8,128)(2,1)} %param.19), channel_id=1, replica_groups=mesh['grp'=2,'seq'=4,'mdl'=2,'pair'=2] {'seq','pair'}, dimensions={0}, use_global_device_ids=true | all-gather | bytes 589824 | tf_op jit(solution)/shard_map/all_gather | solution.py:106
  26.8 14.9 %all_gather.7 = bf16[512,512]{1,0:T(8,128)(2,1)S(1)} all-gather(bf16[64,512]{1,0:T(8,128)(2,1)} %param.20), channel_id=1, replica_groups=mesh['grp'=2,'seq'=4,'mdl'=2,'pair'=2] {'seq','pair'}, dimensions={0}, use_global_device_ids=true | all-gather | bytes 589824 | tf_op jit(solution)/shard_map/all_gather | solution.py:107
  44.6 6.4 %copy.62 = bf16[512,4096]{0,1:T(8,128)(2,1)} copy(bf16[512,4096]{1,0:T(8,128)(2,1)} %param.15) | data formatting | bytes 8388608 | tf_op args[0]
  51.0 6.2 %copy.73 = bf16[4,512,8,128]{3,1,2,0:T(8,128)(2,1)} copy(bf16[4,512,8,128]{1,3,2,0:T(8,128)(2,1)} %bitcast.366) | data formatting | bytes 8388608
  57.5 48.3 %while.33 = (s32[]{:T(128)}, f32[4,512,8,128]{1,3,2,0:T(8,128)}, f32[4,8,512,1]{2,1,3,0:T(8,128)S(1)}, bf16[4,768,128]{1,2,0:T(8,128)(2,1)}, pred[512,768]{0,1:T...) while((s32[]{:T(128)}, f32[4,512,8,128]{1,3,2,0:T(8,128)}, ...), condition=%wide.region_4.5_spmd.clone, body=%wide.region_1.4_spmd.sunk.clone | while | flops 1648357376 | bytes 42600528 | solution.py:82
  57.6 3.6 %fusion.172 = (f32[8,512]{1,0:T(8,128)S(1)}, f32[768,512,8]{1,0,2:T(8,128)S(1)}) fusion(pred[512,768]{0,1:T(8,128)(4,1)S(1)} %get-tuple-element.478, bf16[4,512,8,128]{3,1,2,0:T(8,128)(2,1)} %get-tuple-element.480, s32[]{:T(128)} %get-tuple-element.467, bf16[4,768,128]{1,2,0:T(8,128)(2,1)S(1)} %get-tuple-element.479), kind=kOutput, calls=%fused_computation.6.clone.1.clone | convolution fusion | flops 814739456 | bytes 14238720 | tf_op jit(solution)/shard_map/while/body/eval_jaxpr/rgd,kd->grk/dot_general | solution.py:23
  61.2 2.6 fusion.173
  63.8 5.8 %bitcast_dynamic-update-slice_fusion.9 = f32[4,512,8,128]{1,3,2,0:T(8,128)} fusion(f32[4,512,8,128]{1,3,2,0:T(8,128)} %get-tuple-element.468, s32[]{:T(128)} %get-tuple-element.467, f32[768,512,8]{1,0,2:T(8,128)S(1)} %get-tuple-element.416, f32[8,512]{1,0:T(8,128)S(1)} %fusion.173, f32[8,512]{1,0:T(8,128)S(1)} %get-tuple-element.417, ...), kind=kOutput, calls=%fused_computation.8.clone.1.clone | convolution fusion | flops 821035008 | bytes 15303680 | tf_op jit(solution)/shard_map/while/body/eval_jaxpr/grk,kd->rgd/dot_general | solution.py:23
  69.6 3.6 %fusion.172 = (f32[8,512]{1,0:T(8,128)S(1)}, f32[768,512,8]{1,0,2:T(8,128)S(1)}) fusion(pred[512,768]{0,1:T(8,128)(4,1)S(1)} %get-tuple-element.478, bf16[4,512,8,128]{3,1,2,0:T(8,128)(2,1)} %get-tuple-element.480, s32[]{:T(128)} %get-tuple-element.467, bf16[4,768,128]{1,2,0:T(8,128)(2,1)S(1)} %get-tuple-element.479), kind=kOutput, calls=%fused_computation.6.clone.1.clone | convolution fusion | flops 814739456 | bytes 14238720 | tf_op jit(solution)/shard_map/while/body/eval_jaxpr/rgd,kd->grk/dot_general | solution.py:23
  73.3 2.6 fusion.173
  75.9 5.8 %bitcast_dynamic-update-slice_fusion.9 = f32[4,512,8,128]{1,3,2,0:T(8,128)} fusion(f32[4,512,8,128]{1,3,2,0:T(8,128)} %get-tuple-element.468, s32[]{:T(128)} %get-tuple-element.467, f32[768,512,8]{1,0,2:T(8,128)S(1)} %get-tuple-element.416, f32[8,512]{1,0:T(8,128)S(1)} %fusion.173, f32[8,512]{1,0:T(8,128)S(1)} %get-tuple-element.417, ...), kind=kOutput, calls=%fused_computation.8.clone.1.clone | convolution fusion | flops 821035008 | bytes 15303680 | tf_op jit(solution)/shard_map/while/body/eval_jaxpr/grk,kd->rgd/dot_general | solution.py:23
  81.7 3.6 %fusion.172 = (f32[8,512]{1,0:T(8,128)S(1)}, f32[768,512,8]{1,0,2:T(8,128)S(1)}) fusion(pred[512,768]{0,1:T(8,128)(4,1)S(1)} %get-tuple-element.478, bf16[4,512,8,128]{3,1,2,0:T(8,128)(2,1)} %get-tuple-element.480, s32[]{:T(128)} %get-tuple-element.467, bf16[4,768,128]{1,2,0:T(8,128)(2,1)S(1)} %get-tuple-element.479), kind=kOutput, calls=%fused_computation.6.clone.1.clone | convolution fusion | flops 814739456 | bytes 14238720 | tf_op jit(solution)/shard_map/while/body/eval_jaxpr/rgd,kd->grk/dot_general | solution.py:23
  85.3 2.6 fusion.173
  87.9 5.9 %bitcast_dynamic-update-slice_fusion.9 = f32[4,512,8,128]{1,3,2,0:T(8,128)} fusion(f32[4,512,8,128]{1,3,2,0:T(8,128)} %get-tuple-element.468, s32[]{:T(128)} %get-tuple-element.467, f32[768,512,8]{1,0,2:T(8,128)S(1)} %get-tuple-element.416, f32[8,512]{1,0:T(8,128)S(1)} %fusion.173, f32[8,512]{1,0:T(8,128)S(1)} %get-tuple-element.417, ...), kind=kOutput, calls=%fused_computation.8.clone.1.clone | convolution fusion | flops 821035008 | bytes 15303680 | tf_op jit(solution)/shard_map/while/body/eval_jaxpr/grk,kd->rgd/dot_general | solution.py:23
  93.8 3.6 %fusion.172 = (f32[8,512]{1,0:T(8,128)S(1)}, f32[768,512,8]{1,0,2:T(8,128)S(1)}) fusion(pred[512,768]{0,1:T(8,128)(4,1)S(1)} %get-tuple-element.478, bf16[4,512,8,128]{3,1,2,0:T(8,128)(2,1)} %get-tuple-element.480, s32[]{:T(128)} %get-tuple-element.467, bf16[4,768,128]{1,2,0:T(8,128)(2,1)S(1)} %get-tuple-element.479), kind=kOutput, calls=%fused_computation.6.clone.1.clone | convolution fusion | flops 814739456 | bytes 14238720 | tf_op jit(solution)/shard_map/while/body/eval_jaxpr/rgd,kd->grk/dot_general | solution.py:23
  97.4 2.6 fusion.173
  100.0 5.8 %bitcast_dynamic-update-slice_fusion.9 = f32[4,512,8,128]{1,3,2,0:T(8,128)} fusion(f32[4,512,8,128]{1,3,2,0:T(8,128)} %get-tuple-element.468, s32[]{:T(128)} %get-tuple-element.467, f32[768,512,8]{1,0,2:T(8,128)S(1)} %get-tuple-element.416, f32[8,512]{1,0:T(8,128)S(1)} %fusion.173, f32[8,512]{1,0:T(8,128)S(1)} %get-tuple-element.417, ...), kind=kOutput, calls=%fused_computation.8.clone.1.clone | convolution fusion | flops 821035008 | bytes 15303680 | tf_op jit(solution)/shard_map/while/body/eval_jaxpr/grk,kd->rgd/dot_general | solution.py:23
  105.8 6.4 %copy.69 = bf16[512,4096]{0,1:T(8,128)(2,1)} copy(bf16[512,4096]{1,0:T(8,128)(2,1)} %param.18) | data formatting | bytes 8388608 | tf_op args[3]
  112.2 6.7 %convert_element_type.82 = f32[512,4096]{0,1:T(8,128)} convert(bf16[512,4096]{0,1:T(8,128)(2,1)} %copy.69) | non-fusion elementwise | flops 2097152 | bytes 12582912 | tf_op jit(solution)/shard_map/convert_element_type | solution.py:123
  119.6 6.1 %select_reduce_fusion = f32[]{:T(128)} fusion(f32[4,512,8,128]{1,3,2,0:T(8,128)S(1)} %copy-done.2, f32[4,512,8,128]{1,3,2,0:T(8,128)} %bitcast.364, pred[512]{0:T(512)(128)(4,1)S(1)} %iota_compare_fusion.2), kind=kLoop, calls=%fused_computation.102 | loop fusion | flops 6291455 | bytes 16777732 | tf_op jit(solution)/shard_map/reduce_sum | solution.py:122
  125.8 5.5 %psum.15 = f32[]{:T(128)} all-reduce(f32[]{:T(128)} %select_reduce_fusion), channel_id=1, replica_groups=mesh['grp'=2,'seq'=4,'mdl'=2,'pair'=2] {'mdl'}, use_global_device_ids=true, to_apply=%region_8.9 | all-reduce | flops 1 | bytes 8 | tf_op jit(solution)/shard_map/psum | solution.py:128
  133.7 2.4 broadcast_convert_fusion
  137.0 12.3 %psum.14 = f32[8]{0:T(128)S(1)} all-reduce(f32[8]{0:T(128)S(1)} %compare_select_fusion.1), channel_id=1, replica_groups=mesh['grp'=2,'seq'=4,'mdl'=2,'pair'=2] {'seq'}, use_global_device_ids=true, to_apply=%region_5.6 | all-reduce | flops 8 | bytes 64 | tf_op jit(solution)/shard_map/psum | solution.py:127
  151.9 6.4 %multiply_reduce_fusion = f32[4,512,8]{1,2,0:T(8,128)S(1)} fusion(f32[4,512,8,128]{1,3,2,0:T(8,128)} %get-tuple-element.130, bf16[512,4096]{0,1:T(8,128)(2,1)} %copy.69, f32[]{:T(128)S(6)} %select_n.55, pred[512]{0:T(512)(128)(4,1)S(1)} %iota_compare_fusion.2), kind=kLoop, calls=%fused_computation.100 | loop fusion | flops 10469376 | bytes 12648964 | tf_op jit(solution)/shard_map/reduce_sum | solution.py:139
  158.3 3.1 %multiply_select_fusion = bf16[512,4096]{0,1:T(8,128)(2,1)} fusion(f32[]{:T(128)S(6)} %select_n.55, pred[512]{0:T(512)(128)(4,1)S(1)} %iota_compare_fusion.2, bf16[512,4096]{0,1:T(8,128)(2,1)S(1)} %copy-done.1), kind=kLoop, calls=%fused_computation.101 | loop fusion | flops 6291456 | bytes 8389124 | tf_op jit(solution)/shard_map/jit(_where)/select_n | solution.py:137
  161.4 57.9 %while.34 = (s32[]{:T(128)}, bf16[4,512,8,128]{1,3,2,0:T(8,128)(2,1)}, bf16[4,256,128]{2,1,0:T(8,128)(2,1)S(1)}, bf16[4,256,128]{2,1,0:T(8,128)(2,1)S(1)}, bf16[...) while((s32[]{:T(128)}, ...), condition=%wide.region_11.12_spmd.clone.clone, body=%wide.region_10.11_spmd.clone.sunk.clone | while | flops 4059398144 | bytes 140749072 | solution.py:159
  161.4 2.7 fusion.197
  164.2 2.8 fusion.198
  170.7 1.3 fusion.201
  172.7 1.6 fusion.202
  175.9 2.7 fusion.197
  178.7 2.8 fusion.198
  185.2 1.3 fusion.201
  187.2 1.6 fusion.202
  190.4 2.7 fusion.197
  193.2 2.8 fusion.198
  199.7 1.3 fusion.201
  201.7 1.6 fusion.202
  204.9 2.7 fusion.197
  207.7 2.8 fusion.198
  216.2 1.6 fusion.202
  219.6 2.5 dynamic_update_slice.28
  224.0 6.3 %copy.88 = bf16[512,4096]{1,0:T(8,128)(2,1)} copy(bf16[512,4096]{0,1:T(8,128)(2,1)} %bitcast.365) | data formatting | bytes 8388608 | tf_op jit(solution)/shard_map/convert_element_type | solution.py:188
  232.0 20.5 %reduce-scatter.3.cloned.1.call-done = bf16[64,512]{1,0:T(8,128)(2,1)} async-done(((bf16[512,512]{1,0:T(8,128)(2,1)}), bf16[64,512]{1,0:T(8,128)(2,1)}) %reduce-scatter.3.cloned.1.call-update) | async-done | bytes 65552 | tf_op jit(solution)/shard_map/reduce_scatter | solution.py:180
  252.6 1.5 convert_element_type.79
  254.1 30.0 %reduce-scatter.5.cloned.1.call-done = bf16[64,512]{1,0:T(8,128)(2,1)} async-done(((bf16[512,512]{1,0:T(8,128)(2,1)}), bf16[64,512]{1,0:T(8,128)(2,1)}) %reduce-scatter.5.cloned.1.call-update) | async-done | bytes 65552 | tf_op jit(solution)/shard_map/reduce_scatter | solution.py:183
  284.1 1.5 convert_element_type.80
  (115 shorter events, 34.2 us)
Async XLA Ops:
  7.2 37.4 %copy-start.7 = (s32[512]{0:T(512)S(1)}, s32[512]{0:T(512)}, u32[]{:S(2)}) copy-start(s32[512]{0:T(512)} %param.21) | copy-start | bytes 6148
  7.2 36.1 %copy-start.6 = (bf16[512,512]{1,0:T(8,128)(2,1)S(1)}, bf16[512,512]{1,0:T(8,128)(2,1)}, u32[]{:S(2)}) copy-start(bf16[512,512]{1,0:T(8,128)(2,1)} %param.17) | copy-start | bytes 1572868
  7.2 245.4 %reduce-scatter.3.cloned.1.call-start = ((), (), s32[]{:S(2)}) async-start(), calls=%async_computation.2 | async-start | bytes 589824 | tf_op jit(solution)/shard_map/reduce_scatter | solution.py:180
  44.6 12.7 %copy-start.8 = (pred[256]{0:T(512)(128)(4,1)}, pred[256]{0:T(512)(128)(4,1)S(1)}, u32[]{:S(2)}) copy-start(pred[256]{0:T(512)(128)(4,1)S(1)} %dynamic-slice_compare_fusion) | copy-start | bytes 772
  112.2 7.4 %copy-start.2 = (f32[4,512,8,128]{1,3,2,0:T(8,128)S(1)}, f32[4,512,8,128]{1,3,2,0:T(8,128)}, u32[]{:S(2)}) copy-start(f32[4,512,8,128]{1,3,2,0:T(8,128)} %get-tuple-element.130) | copy-start | bytes 25165828
  132.6 18.0 %collective-permute-start = (f32[]{:T(128)}, f32[]{:T(128)}, u32[]{:S(2)}, u32[]{:S(2)}) collective-permute-start(f32[]{:T(128)} %sub.50), channel_id=1, source_target_pairs={{0,1},{1,0},{2,3},{3,2},{4,5},{5,4},{6,7},{7,6},{8,9},{9,8},{10,11... | collective-permute-start | bytes 20 | tf_op jit(solution)/shard_map/ppermute | solution.py:19
  151.9 6.4 %copy-start.1 = (bf16[512,4096]{0,1:T(8,128)(2,1)S(1)}, bf16[512,4096]{0,1:T(8,128)(2,1)}, u32[]{:S(2)}) copy-start(bf16[512,4096]{0,1:T(8,128)(2,1)} %copy.69) | copy-start | bytes 12582916
  158.3 3.1 %copy-start.9 = (pred[256]{0:T(512)(128)(4,1)S(1)}, pred[256]{0:T(512)(128)(4,1)}, u32[]{:S(2)}) copy-start(pred[256]{0:T(512)(128)(4,1)} %copy-done.8) | copy-start | bytes 772
  161.4 2.8 copy-start.5
  164.2 2.8 copy-start
  167.8 2.2 copy-start.3
  170.7 2.0 copy-start.4
  175.9 2.8 copy-start.5
  178.7 2.8 copy-start
  182.3 2.2 copy-start.3
  185.2 2.0 copy-start.4
  190.4 2.8 copy-start.5
  193.2 2.8 copy-start
  196.8 2.2 copy-start.3
  199.7 2.0 copy-start.4
  204.9 2.8 copy-start.5
  207.7 2.8 copy-start
  211.3 2.2 copy-start.3
  214.2 2.0 copy-start.4
  223.2 60.8 %reduce-scatter.5.cloned.1.call-start = ((), (), s32[]{:S(2)}) async-start(), calls=%async_computation.3 | async-start | bytes 589824 | tf_op jit(solution)/shard_map/reduce_scatter | solution.py:183
Sparse Core Ops, SparseCore 0:
  223.4 29.1 reduce-scatter.2
  254.9 29.1 reduce-scatter.4
where the time goes:
time: 294 us; the launch traced here: 292 us
  matrix products  90.6 us (31%)
  waiting for transfers between devices  51.3 us (17%)
  blocking collectives  49.6 us (17%)
  other arithmetic  41 us (14%)
  local copies, waits for them, and re-layouts  38.3 us (13%)
  between operations  20.2 us (7%)
    dot_general x48, matrix products, product(): return jnp.einsum(form, left, right, preferred_element_type=jnp.float32)  90.6 us
    reduce_scatter x1, waiting for transfers between devices, per_device(): lax.psum_scatter(placed[:, width:].astype(jnp.bfloat16), ('seq', 'pair'),...  30 us
    unnamed x19, local copies, waits for them, and re-layouts  20.8 us
    reduce_scatter x1, waiting for transfers between devices, per_device(): lax.psum_scatter(placed[:, :width].astype(jnp.bfloat16), ('seq', 'pair'),...  20.5 us
    all_gather x1, blocking collectives, per_device(): lax.all_gather(packed_prompt_key, ('seq', 'pair'), axis=0, tiled=True)  16.8 us
    all_gather x1, blocking collectives, per_device(): lax.all_gather(packed_prompt_value, ('seq', 'pair'), axis=0, tiled=True)  14.9 us
    psum x1, blocking collectives, per_device(): lax.psum(jnp.where(domain_slots == domain_of[0], 1.0, 0.0).astype(jnp.flo...  12.3 us
    reduce_sum x4, other arithmetic, head_forward(): row_sum = jnp.sum(exponent, axis=-1, keepdims=True)  10.3 us
  transfers between devices with their start and end apart: 3, of which 2 were waited for; matrix products, arithmetic and copies ran while one was open for 4% of the time, Pallas kernels for 0%

commit v1 on v0

v1 whole, which is shorter than its diff:
```python
import functools
import math

import jax
import jax.numpy as jnp
from jax import lax
from jax.experimental import pallas as pl
from jax.experimental.pallas import tpu as pltpu
from jax.sharding import PartitionSpec as P

HEAD_SIZE = 128
PROMPT_DEV = 64
BLK = 128
NDOM = 8
WINDOW = 4 * PROMPT_DEV
NEG = -1e30

dpo_beta = 0.5
loss_scale = 256.0


def dot(left, right, left_dim, right_dim):
    return lax.dot_general(
        left, right, (((left_dim,), (right_dim,)), ((), ())), preferred_element_type=jnp.float32
    )


def head_chain(rb, heads, q_ref, r_ref, dq_ref, lp_ref, kcat, vcat, kt, bias, tri, dkacc, dvacc):
    scale = HEAD_SIZE**-0.5
    log_scale = scale * math.log2(math.e)
    seen = WINDOW + BLK * (rb + 1)
    rows = slice(rb * BLK, (rb + 1) * BLK)
    queries = jnp.concatenate([q_ref[rows, h * HEAD_SIZE : (h + 1) * HEAD_SIZE] for h in heads], axis=0)
    reads = jnp.concatenate([r_ref[rows, h * HEAD_SIZE : (h + 1) * HEAD_SIZE] for h in heads], axis=0)
    scores = dot(kcat[:seen, :], queries, 1, 1)
    dprob = dot(vcat[:seen, :], reads, 1, 1)
    wide = len(heads)
    prompt_bias = jnp.concatenate([bias[...]] * wide, axis=1)
    diagonal = jnp.concatenate([tri[...]] * wide, axis=1)
    parts = [scores[:WINDOW] + prompt_bias]
    if rb:
        parts.append(scores[WINDOW : seen - BLK])
    parts.append(scores[seen - BLK :] + diagonal)
    scores = jnp.concatenate(parts, axis=0)
    top = jnp.max(scores, axis=0, keepdims=True) * log_scale
    exponent = jnp.exp2(scores * log_scale - top)
    inverse = 1.0 / jnp.sum(exponent, axis=0, keepdims=True)
    row_dot = jnp.sum(exponent * dprob, axis=0, keepdims=True) * inverse
    weights = exponent * inverse
    dscore = (weights * (dprob - row_dot)).astype(jnp.bfloat16)
    weights = weights.astype(jnp.bfloat16)
    dvacc[:seen, :] += dot(weights, reads, 1, 0)
    dkacc[:seen, :] += dot(dscore, queries, 1, 0)
    dq = (dot(kt[:, :seen], dscore, 1, 0) * scale).T.astype(jnp.bfloat16)
    for n, h in enumerate(heads):
        dq_ref[rows, h * HEAD_SIZE : (h + 1) * HEAD_SIZE] = dq[n * BLK : (n + 1) * BLK]
        lp_ref[0:1, :] += row_dot[:, n * BLK : (n + 1) * BLK]


def attention_kernel(
    group, at_once, blocks_ref, slot_ref, owner_ref, q_ref, r_ref, k_ref, v_ref, gk_ref, gv_ref,
    dq_ref, dk_ref, dv_ref, pk_ref, pv_ref, lp_ref,
    sel, bias, tri, kcat, vcat, kt, dkacc, dvacc,
):
    @pl.when(pl.program_id(0) == 0)
    def _():
        owner = owner_ref[...]
        slot = slot_ref[0]
        first = jnp.sum(jnp.where(owner < slot, 1.0, 0.0), axis=1, keepdims=True).astype(jnp.int32)
        column = lax.broadcasted_iota(jnp.int32, sel.shape, 1)
        row = lax.broadcasted_iota(jnp.int32, sel.shape, 0)
        chosen = jnp.where((column - row == first) & (owner == slot), 1.0, 0.0)
        sel[...] = chosen.astype(jnp.bfloat16)
        shown = jnp.sum(chosen, axis=1, keepdims=True)
        bias[...] = jnp.broadcast_to(jnp.where(shown > 0.5, 0.0, NEG), bias.shape)
        key = lax.broadcasted_iota(jnp.int32, tri.shape, 0)
        query = lax.broadcasted_iota(jnp.int32, tri.shape, 1)
        tri[...] = jnp.where(key > query, NEG, 0.0)
        lp_ref[...] = jnp.zeros_like(lp_ref)

    kcat[:WINDOW, :] = dot(sel[...], gk_ref[...], 1, 0).astype(jnp.bfloat16)
    vcat[:WINDOW, :] = dot(sel[...], gv_ref[...], 1, 0).astype(jnp.bfloat16)
    kcat[WINDOW:, :] = k_ref[...]
    vcat[WINDOW:, :] = v_ref[...]
    kt[...] = kcat[...].T
    dkacc[...] = jnp.zeros_like(dkacc)
    dvacc[...] = jnp.zeros_like(dvacc)
    for rb in range(q_ref.shape[0] // BLK):

        @pl.when(rb < blocks_ref[0])
        def _():
            for start in range(0, group, at_once):
                head_chain(
                    rb, list(range(start, start + at_once)), q_ref, r_ref, dq_ref, lp_ref,
                    kcat, vcat, kt, bias, tri, dkacc, dvacc,
                )

        @pl.when(rb >= blocks_ref[0])
        def _():
            dq_ref[rb * BLK : (rb + 1) * BLK, :] = jnp.zeros((BLK, dq_ref.shape[1]), dq_ref.dtype)

    scale = HEAD_SIZE**-0.5
    dk_ref[...] = (dkacc[WINDOW:, :] * scale).astype(dk_ref.dtype)
    dv_ref[...] = dvacc[WINDOW:, :].astype(dv_ref.dtype)
    pk_ref[...] = dot(sel[...], (dkacc[:WINDOW, :] * scale).astype(jnp.bfloat16), 0, 0).astype(pk_ref.dtype)
    pv_ref[...] = dot(sel[...], dvacc[:WINDOW, :].astype(jnp.bfloat16), 0, 0).astype(pv_ref.dtype)


def attention(q, r, k, v, gk, gv, owner, slot, blocks):
    rows, columns = q.shape
    tokens = gk.shape[0]
    heads = k.shape[1] // HEAD_SIZE
    group = columns // k.shape[1]
    wide = pl.BlockSpec((rows, group * HEAD_SIZE), lambda g: (0, g))
    slim = pl.BlockSpec((rows, HEAD_SIZE), lambda g: (0, g))
    packed = pl.BlockSpec((tokens, HEAD_SIZE), lambda g: (0, g))
    smem = pl.BlockSpec(memory_space=pltpu.SMEM)
    keys = WINDOW + rows
    bf16, f32 = jnp.bfloat16, jnp.float32
    return pl.pallas_call(
        functools.partial(attention_kernel, group, 2),
        grid=(heads,),
        in_specs=[smem, smem, pl.BlockSpec((1, tokens), lambda g: (0, 0)), wide, wide, slim, slim, packed, packed],
        out_specs=[wide, slim, slim, packed, packed, pl.BlockSpec((8, BLK), lambda g: (0, 0))],
        out_shape=[
            jax.ShapeDtypeStruct((rows, columns), bf16),
            jax.ShapeDtypeStruct(k.shape, bf16),
            jax.ShapeDtypeStruct(k.shape, bf16),
            jax.ShapeDtypeStruct(gk.shape, bf16),
            jax.ShapeDtypeStruct(gk.shape, bf16),
            jax.ShapeDtypeStruct((8, BLK), f32),
        ],
        scratch_shapes=[
            pltpu.VMEM((WINDOW, tokens), bf16),
            pltpu.VMEM((WINDOW, HEAD_SIZE), f32),
            pltpu.VMEM((BLK, BLK), f32),
            pltpu.VMEM((keys, HEAD_SIZE), bf16),
            pltpu.VMEM((keys, HEAD_SIZE), bf16),
            pltpu.VMEM((HEAD_SIZE, keys), bf16),
            pltpu.VMEM((keys, HEAD_SIZE), f32),
            pltpu.VMEM((keys, HEAD_SIZE), f32),
        ],
        compiler_params=pltpu.CompilerParams(vmem_limit_bytes=48 * 1024 * 1024),
        cost_estimate=pl.CostEstimate(flops=12 * 10**9, bytes_accessed=16 * 2**20, transcendentals=10**7),
        name="attention_gradients",
    )(blocks, slot, owner, q, r, k, v, gk, gv)


def per_device(
    resp_query, resp_key, response_value, readout, packed_prompt_key, packed_prompt_value,
    prompt_owner, pair_slot, domain_of, resp_blocks, ref_logprob,
):
    seq_count = lax.axis_size("seq")
    width = packed_prompt_key.shape[1]
    packed = jnp.concatenate([packed_prompt_key, packed_prompt_value], axis=1)
    gathered = lax.all_gather(packed, ("seq", "pair"), axis=0, tiled=True)
    dq, dk, dv, pk, pv, lp = attention(
        resp_query, readout, resp_key, response_value, gathered[:, :width], gathered[:, width:],
        prompt_owner[None, :], pair_slot, resp_blocks,
    )
    side = lax.axis_index("pair")
    domain_slots = jnp.arange(NDOM)
    counts = lax.psum(jnp.where(domain_slots == domain_of[0], 1.0, 0.0).astype(jnp.float32), "seq")
    own_gap = lax.psum(jnp.sum(lp[0]), "mdl") - ref_logprob[0]
    other_gap = lax.ppermute(own_gap, "pair", [(0, 1), (1, 0)])
    sign = jnp.where(side == 0, 1.0, -1.0)
    margin = dpo_beta * sign * (own_gap - other_gap)
    own_count = jnp.sum(jnp.where(domain_slots == domain_of[0], counts, 0.0))
    weight = seq_count / (NDOM * own_count)
    coef = -sign * loss_scale * weight * dpo_beta * jax.nn.sigmoid(-margin)
    placed = (jnp.concatenate([pk, pv], axis=1).astype(jnp.float32) * coef).astype(jnp.bfloat16)
    summed = lax.psum_scatter(placed, ("seq", "pair"), scatter_dimension=0, tiled=True).astype(jnp.float32)

    def scaled(array):
        return (array.astype(jnp.float32) * coef).astype(jnp.bfloat16)

    return scaled(dq), scaled(dk), scaled(dv), summed[:, :width], summed[:, width:]


def solution(mesh):
    tokens = P(("grp", "seq", "pair"), "mdl")
    each = P(("grp", "seq", "pair"))
    in_specs = (tokens,) * 6 + (P("grp"), P(("grp", "seq")), P(("grp", "seq")), each, each)
    return jax.shard_map(per_device, mesh=mesh, in_specs=in_specs, out_specs=(tokens,) * 5, check_vma=False)
```

time: 294 us -> 143 us (0.49)
  matrix products: 90.6 us -> 0 us
  Pallas kernels: 0 us -> 38.2 us
  local copies, waits for them, and re-layouts: 38.3 us -> 5.62 us
  other arithmetic: 41 us -> 10.4 us
  blocking collectives: 49.6 us -> 19 us
    dot_general x48 -> x0, matrix products: 90.6 us -> none  [product(): return jnp.einsum(form, left, right, preferred_element_type=jnp.float32)]
    pallas_call x0 -> x1, Pallas kernels: none -> 38.2 us  [attention(): pl.pallas_call(functools.partial(attention_kernel, group, 2), grid=(heads...]
    all_gather x2 -> x0, blocking collectives: 31.7 us -> none  [the longest x1 16.8 us: per_device(): lax.all_gather(packed_prompt_key, ('seq', 'pair'), axis=0, tiled=True)]
    reduce_sum x7 -> x1, other arithmetic: 24.2 us -> 0.6 us  [per_device(): own_gap = lax.psum(jnp.sum(lp[0]), 'mdl') - ref_logprob[0]]
    unnamed x19 -> x6, local copies, waits for them, and re-layouts: 20.8 us -> 2.76 us
    reduce_scatter x2 -> x1, waiting for transfers between devices: 50.5 us -> 40.1 us  [per_device(): lax.psum_scatter(placed, ('seq', 'pair'), scatter_dimension=0, tiled=True)]
    all_gather x0 -> x1, waiting for transfers between devices: none -> 8.85 us  [per_device(): gathered = lax.all_gather(packed, ('seq', 'pair'), axis=0, tiled=True)]
    convert_element_type x3 -> x0, local copies, waits for them, and re-layouts: 8.03 us -> none  [the longest x1 6.33 us: per_device(): query_grad.astype(jnp.bfloat16)]
  transfers between devices with their start and end apart: 3 -> 3, of which waited for: 2 -> 3; matrix products, arithmetic and copies ran while one was open for 4% -> 5% of each run, Pallas kernels for 0% -> 0%
where the time goes in v1:
time: 143 us; the launch traced here: 142 us
  waiting for transfers between devices  49.3 us (34%)
  Pallas kernels  38.2 us (27%)
  blocking collectives  19 us (13%)
  between operations  18.8 us (13%)
  other arithmetic  10.4 us (7%)
  local copies, waits for them, and re-layouts  5.62 us (4%)
    reduce_scatter x1, waiting for transfers between devices, per_device(): lax.psum_scatter(placed, ('seq', 'pair'), scatter_dimension=0, tiled=True)  40.1 us
    pallas_call x1, Pallas kernels, attention(): pl.pallas_call(functools.partial(attention_kernel, group, 2), grid=(heads...  38.2 us
    psum x1, blocking collectives, per_device(): lax.psum(jnp.where(domain_slots == domain_of[0], 1.0, 0.0).astype(jnp.flo...  13.5 us
    all_gather x1, waiting for transfers between devices, per_device(): gathered = lax.all_gather(packed, ('seq', 'pair'), axis=0, tiled=True)  8.85 us
    convert_element_type x2, other arithmetic, scaled(): return (array.astype(jnp.float32) * coef).astype(jnp.bfloat16)  6.4 us
    psum x1, blocking collectives, per_device(): own_gap = lax.psum(jnp.sum(lp[0]), 'mdl') - ref_logprob[0]  5.55 us
  transfers between devices with their start and end apart: 3, of which 3 were waited for; matrix products, arithmetic and copies ran while one was open for 5% of the time, Pallas kernels for 0%

profile of v1, /device:TPU:0, one launch (start us, length us, event | category | flops | bytes accessed | tf_op | source)
XLA Modules:
  0.0 142.3 jit_solution(1002616630213752570)
XLA Ops:
  7.2 0.0 all-gather.2.cloned.1.call-start
  7.2 1.5 %pad_maximum_fusion = bf16[64,1024]{1,0:T(8,128)(2,1)} fusion(bf16[64,512]{1,0:T(8,128)(2,1)} %param.16, bf16[64,512]{1,0:T(8,128)(2,1)} %param.15), kind=kLoop, calls=%fused_computation.4 | loop fusion | flops 262144 | bytes 262144 | tf_op jit(solution)/shard_map/concatenate | solution.py:155
  8.7 0.0 all-gather.2.cloned.1.call-update
  8.8 0.0 reduce-scatter.2.cloned.1.call-start
  9.5 13.5 %psum.14 = f32[8]{0:T(128)S(1)} all-reduce(f32[8]{0:T(128)S(1)} %compare_select_fusion.1), channel_id=1, replica_groups=mesh['grp'=2,'seq'=4,'mdl'=2,'pair'=2] {'seq'}, use_global_device_ids=true, to_apply=%region_0.1 | all-reduce | flops 8 | bytes 64 | tf_op jit(solution)/shard_map/psum | solution.py:163
  24.9 0.6 fusion
  26.2 8.9 %all-gather.2.cloned.1.call-done = bf16[512,1024]{1,0:T(8,128)(2,1)} async-done(((bf16[64,1024]{1,0:T(8,128)(2,1)}), bf16[512,1024]{1,0:T(8,128)(2,1)}) %all-gather.2.cloned.1.call-update) | async-done | bytes 1048592 | tf_op jit(solution)/shard_map/all_gather | solution.py:156
  35.0 1.3 fusion.1
  36.3 0.0 copy-start
  36.3 1.0 copy-done
  37.4 0.0 copy-start.1
  37.4 1.0 copy-done.1
  38.4 0.0 copy-start.2
  38.4 0.7 copy-done.2
  39.1 38.2 %attention_gradients.1 = (bf16[512,4096]{1,0:T(8,128)(2,1)}, bf16[512,512]{1,0:T(8,128)(2,1)S(1)}, bf16[512,512]{1,0:T(8,128)(2,1)S(1)}, bf16[512,512]{1,0:T(8,1...) custom-call(s32[1]{0:T(128)S(6)} %copy.18.blocks_ref, s32[1]{0:T(128)S(6)} %copy.16.slot_ref, ...), custom_call_target="tpu_custom_call" | custom-call | flops 12000000000 | bytes 16777216 | tf_op jit(solution)/shard_map/attention_gradients/pallas_call | solution.py:120
  77.3 0.6 slice_reduce_fusion
  77.9 5.5 %psum.15 = f32[]{:T(128)} all-reduce(f32[]{:T(128)} %slice_reduce_fusion), channel_id=1, replica_groups=mesh['grp'=2,'seq'=4,'mdl'=2,'pair'=2] {'mdl'}, use_global_device_ids=true, to_apply=%region_3.4 | all-reduce | flops 1 | bytes 8 | tf_op jit(solution)/shard_map/psum | solution.py:164
  84.1 0.9 collective-permute-start
  85.0 0.3 collective-permute-done
  86.1 1.2 multiply_convert_fusion.1
  87.3 0.0 reduce-scatter.2.cloned.1.call-update
  87.3 1.2 multiply_convert_fusion.2
  88.5 5.2 %multiply_convert_fusion = bf16[512,4096]{1,0:T(8,128)(2,1)} fusion(bf16[512,4096]{1,0:T(8,128)(2,1)} %get-tuple-element.11, f32[]{:T(128)S(6)} %mul.45), kind=kLoop, calls=%fused_computation | loop fusion | flops 6291456 | bytes 8388612 | tf_op jit(solution)/shard_map/convert_element_type | solution.py:175
  93.7 40.1 %reduce-scatter.2.cloned.1.call-done = bf16[64,1024]{1,0:T(8,128)(2,1)} async-done(((bf16[512,1024]{1,0:T(8,128)(2,1)}), bf16[64,1024]{1,0:T(8,128)(2,1)}) %reduce-scatter.2.cloned.1.call-update) | async-done | bytes 131088 | tf_op jit(solution)/shard_map/reduce_scatter | solution.py:172
  133.8 1.6 %fusion.2 = (f32[64,512]{1,0:T(8,128)}, f32[64,512]{1,0:T(8,128)}) fusion(bf16[64,1024]{1,0:T(8,128)(2,1)} %reduce-scatter.2.cloned.1.call-done), kind=kLoop, calls=%fused_computation.10 | loop fusion | bytes 524288 | tf_op jit(solution)/shard_map/slice | solution.py:177
  (1 shorter events, 0.0 us)
Async XLA Ops:
  7.2 27.9 %all-gather.2.cloned.1.call-start = ((), (), s32[]{:S(2)}) async-start(), calls=%async_computation.1 | async-start | bytes 1179648 | tf_op jit(solution)/shard_map/all_gather | solution.py:156
  8.8 125.1 %reduce-scatter.2.cloned.1.call-start = ((), (), s32[]{:S(2)}) async-start(), calls=%async_computation.2 | async-start | bytes 1179648 | tf_op jit(solution)/shard_map/reduce_scatter | solution.py:172
  36.3 1.0 copy-start
  37.4 1.0 copy-start.1
  38.4 0.7 copy-start.2
  84.1 1.2 collective-permute-start
Sparse Core Ops, SparseCore 0:
  10.2 24.8 all-gather.1
  87.4 46.3 reduce-scatter.1

commit v2 on v1

v2 whole, which is shorter than its diff:
```python
import functools
import math

import jax
import jax.numpy as jnp
from jax import lax
from jax.experimental import pallas as pl
from jax.experimental.pallas import tpu as pltpu
from jax.sharding import PartitionSpec as P

HEAD_SIZE = 128
PROMPT_DEV = 64
BLK = 128
NDOM = 8
WINDOW = 4 * PROMPT_DEV
NEG = -1e30
AT_ONCE = 2

dpo_beta = 0.5
loss_scale = 256.0


def dot(left, right, left_dim, right_dim):
    return lax.dot_general(
        left, right, (((left_dim,), (right_dim,)), ((), ())), preferred_element_type=jnp.float32
    )


def open_chain(rb, heads, q_ref, r_ref, kcat, vcat):
    seen = WINDOW + BLK * (rb + 1)
    rows = slice(rb * BLK, (rb + 1) * BLK)
    queries = jnp.concatenate([q_ref[rows, h * HEAD_SIZE : (h + 1) * HEAD_SIZE] for h in heads], axis=0)
    reads = jnp.concatenate([r_ref[rows, h * HEAD_SIZE : (h + 1) * HEAD_SIZE] for h in heads], axis=0)
    return queries, reads, dot(kcat[:seen, :], queries, 1, 1), dot(vcat[:seen, :], reads, 1, 1)


def weigh_chain(rb, heads, state, blocks, bias, tri):
    queries, reads, scores, dprob = state
    log_scale = HEAD_SIZE**-0.5 * math.log2(math.e)
    seen = WINDOW + BLK * (rb + 1)
    wide = len(heads)
    parts = [scores[:WINDOW] + jnp.concatenate([bias[...]] * wide, axis=1)]
    if rb:
        parts.append(scores[WINDOW : seen - BLK])
    parts.append(scores[seen - BLK :] + jnp.concatenate([tri[...]] * wide, axis=1))
    scores = jnp.concatenate(parts, axis=0)
    top = jnp.max(scores, axis=0, keepdims=True) * log_scale
    exponent = jnp.exp2(scores * log_scale - top)
    inverse = jnp.where(rb < blocks, 1.0, 0.0) / jnp.sum(exponent, axis=0, keepdims=True)
    row_dot = jnp.sum(exponent * dprob, axis=0, keepdims=True) * inverse
    weights = exponent * inverse
    dscore = (weights * (dprob - row_dot)).astype(jnp.bfloat16)
    return queries, reads, weights.astype(jnp.bfloat16), dscore, row_dot


def close_chain(rb, heads, state, dq_ref, lp_ref, kt, dkacc, dvacc):
    queries, reads, weights, dscore, row_dot = state
    seen = WINDOW + BLK * (rb + 1)
    rows = slice(rb * BLK, (rb + 1) * BLK)
    dvacc[:seen, :] += dot(weights, reads, 1, 0)
    dkacc[:seen, :] += dot(dscore, queries, 1, 0)
    dq = (dot(kt[:, :seen], dscore, 1, 0) * HEAD_SIZE**-0.5).T.astype(jnp.bfloat16)
    for n, h in enumerate(heads):
        dq_ref[rows, h * HEAD_SIZE : (h + 1) * HEAD_SIZE] = dq[n * BLK : (n + 1) * BLK]
        lp_ref[0:1, :] += row_dot[:, n * BLK : (n + 1) * BLK]


def run_chains(chains, blocks, q_ref, r_ref, dq_ref, lp_ref, kcat, vcat, kt, bias, tri, dkacc, dvacc):
    opened = open_chain(*chains[0], q_ref, r_ref, kcat, vcat)
    weighed = None
    for n, chain in enumerate(chains):
        following = open_chain(*chains[n + 1], q_ref, r_ref, kcat, vcat) if n + 1 < len(chains) else None
        done = weigh_chain(*chain, opened, blocks, bias, tri)
        if weighed is not None:
            close_chain(*chains[n - 1], weighed, dq_ref, lp_ref, kt, dkacc, dvacc)
        opened, weighed = following, done
    close_chain(*chains[-1], weighed, dq_ref, lp_ref, kt, dkacc, dvacc)


def attention_kernel(
    group, at_once, blocks_ref, slot_ref, domain_ref, ref_ref, owner_ref, q_ref, r_ref, k_ref, v_ref, gk_ref, gv_ref,
    dq_ref, dk_ref, dv_ref, pk_ref, pv_ref, lp_ref,
    sel, bias, tri, kcat, vcat, kt, dkacc, dvacc,
):
    @pl.when(pl.program_id(0) == 0)
    def _():
        owner = owner_ref[...]
        slot = slot_ref[0]
        first = jnp.sum(jnp.where(owner < slot, 1.0, 0.0), axis=1, keepdims=True).astype(jnp.int32)
        column = lax.broadcasted_iota(jnp.int32, sel.shape, 1)
        row = lax.broadcasted_iota(jnp.int32, sel.shape, 0)
        chosen = jnp.where((column - row == first) & (owner == slot), 1.0, 0.0)
        sel[...] = chosen.astype(jnp.bfloat16)
        shown = jnp.sum(chosen, axis=1, keepdims=True)
        bias[...] = jnp.broadcast_to(jnp.where(shown > 0.5, 0.0, NEG), bias.shape)
        key = lax.broadcasted_iota(jnp.int32, tri.shape, 0)
        query = lax.broadcasted_iota(jnp.int32, tri.shape, 1)
        tri[...] = jnp.where(key > query, NEG, 0.0)
        line = lax.broadcasted_iota(jnp.int32, lp_ref.shape, 0)
        domain = jnp.full(lp_ref.shape, domain_ref[0], jnp.int32).astype(jnp.float32)
        lp_ref[...] = jnp.where(line == 1, ref_ref[0], jnp.where(line == 2, domain, 0.0))

    kcat[:WINDOW, :] = dot(sel[...], gk_ref[...], 1, 0).astype(jnp.bfloat16)
    vcat[:WINDOW, :] = dot(sel[...], gv_ref[...], 1, 0).astype(jnp.bfloat16)
    kcat[WINDOW:, :] = k_ref[...]
    vcat[WINDOW:, :] = v_ref[...]
    kt[...] = kcat[...].T
    dkacc[...] = jnp.zeros_like(dkacc)
    dvacc[...] = jnp.zeros_like(dvacc)
    chains = [(rb, tuple(range(start, start + at_once))) for rb in range(q_ref.shape[0] // BLK) for start in range(0, group, at_once)]
    run_chains(chains, blocks_ref[0], q_ref, r_ref, dq_ref, lp_ref, kcat, vcat, kt, bias, tri, dkacc, dvacc)
    scale = HEAD_SIZE**-0.5
    dk_ref[...] = (dkacc[WINDOW:, :] * scale).astype(dk_ref.dtype)
    dv_ref[...] = dvacc[WINDOW:, :].astype(dv_ref.dtype)
    pk_ref[...] = dot(sel[...], (dkacc[:WINDOW, :] * scale).astype(jnp.bfloat16), 0, 0).astype(pk_ref.dtype)
    pv_ref[...] = dot(sel[...], dvacc[:WINDOW, :].astype(jnp.bfloat16), 0, 0).astype(pv_ref.dtype)


def attention(q, r, k, v, packed_kv, owner, slot, blocks, domain, ref):
    rows, columns = q.shape
    tokens = packed_kv.shape[0]
    heads = k.shape[1] // HEAD_SIZE
    group = columns // k.shape[1]
    wide = pl.BlockSpec((rows, group * HEAD_SIZE), lambda g: (0, g))
    slim = pl.BlockSpec((rows, HEAD_SIZE), lambda g: (0, g))
    packed = pl.BlockSpec((tokens, HEAD_SIZE), lambda g: (0, g))
    packed_value = pl.BlockSpec((tokens, HEAD_SIZE), lambda g: (0, heads + g))
    smem = pl.BlockSpec(memory_space=pltpu.SMEM)
    keys = WINDOW + rows
    bf16, f32 = jnp.bfloat16, jnp.float32
    return pl.pallas_call(
        functools.partial(attention_kernel, group, AT_ONCE),
        grid=(heads,),
        in_specs=[smem] * 4
        + [pl.BlockSpec((1, tokens), lambda g: (0, 0)), wide, wide, slim, slim, packed, packed_value],
        out_specs=[wide, slim, slim, packed, packed, pl.BlockSpec((8, BLK), lambda g: (0, 0))],
        out_shape=[
            jax.ShapeDtypeStruct((rows, columns), bf16),
            jax.ShapeDtypeStruct(k.shape, bf16),
            jax.ShapeDtypeStruct(k.shape, bf16),
            jax.ShapeDtypeStruct((tokens, k.shape[1]), bf16),
            jax.ShapeDtypeStruct((tokens, k.shape[1]), bf16),
            jax.ShapeDtypeStruct((8, BLK), f32),
        ],
        scratch_shapes=[
            pltpu.VMEM((WINDOW, tokens), bf16),
            pltpu.VMEM((WINDOW, HEAD_SIZE), f32),
            pltpu.VMEM((BLK, BLK), f32),
            pltpu.VMEM((keys, HEAD_SIZE), bf16),
            pltpu.VMEM((keys, HEAD_SIZE), bf16),
            pltpu.VMEM((HEAD_SIZE, keys), bf16),
            pltpu.VMEM((keys, HEAD_SIZE), f32),
            pltpu.VMEM((keys, HEAD_SIZE), f32),
        ],
        compiler_params=pltpu.CompilerParams(vmem_limit_bytes=48 * 1024 * 1024),
        cost_estimate=pl.CostEstimate(flops=12 * 10**9, bytes_accessed=16 * 2**20, transcendentals=10**7),
        name="attention_gradients",
    )(blocks, slot, domain, ref, owner, q, r, k, v, packed_kv, packed_kv)


def enter(peers):
    barrier = pltpu.get_barrier_semaphore()
    for peer in peers:
        pl.semaphore_signal(barrier, inc=1, device_id=peer, device_id_type=pl.DeviceIdType.MESH)
    pl.semaphore_wait(barrier, len(peers))


def remote(source, target, send_sem, recv_sem, peer):
    return pltpu.make_async_remote_copy(
        src_ref=source, dst_ref=target, send_sem=send_sem, recv_sem=recv_sem,
        device_id=peer, device_id_type=pl.DeviceIdType.MESH,
    )


def gather_kernel(seq, k_ref, v_ref, out_ref, line_send, line_recv, pair_send, pair_recv):
    me, core = lax.axis_index("seq"), lax.axis_index("pair")
    width = k_ref.shape[1]
    own = me * 2 + core
    out_ref[own, :, :width] = k_ref[...]
    out_ref[own, :, width:] = v_ref[...]
    line = [{"seq": lax.rem(me + off, seq)} for off in range(1, seq)]
    partner = {"pair": 1 - core}
    enter(line + [partner])
    away, across = [], []
    for n in range(seq - 1):
        away.append(remote(out_ref.at[own], out_ref.at[own], line_send.at[n], line_recv.at[n], line[n]))
        away[n].start()
    across.append(remote(out_ref.at[own], out_ref.at[own], pair_send.at[0], pair_recv.at[0], partner))
    across[0].start()
    for n in range(seq - 1):
        away[n].wait_recv()
        held = lax.rem(me + seq - n - 1, seq) * 2 + core
        across.append(remote(out_ref.at[held], out_ref.at[held], pair_send.at[n + 1], pair_recv.at[n + 1], partner))
        across[n + 1].start()
    for copy in across:
        copy.wait()
    for copy in away:
        copy.wait_send()


def gather(k, v):
    seq = lax.axis_size("seq")
    rows, width = k.shape
    dma = pltpu.SemaphoreType.DMA
    out = pl.pallas_call(
        functools.partial(gather_kernel, seq),
        out_shape=jax.ShapeDtypeStruct((2 * seq, rows, 2 * width), k.dtype),
        in_specs=[pl.BlockSpec(memory_space=pltpu.VMEM)] * 2,
        out_specs=pl.BlockSpec(memory_space=pltpu.VMEM),
        scratch_shapes=[dma((seq,)), dma((seq,)), dma((seq,)), dma((seq,))],
        compiler_params=pltpu.CompilerParams(
            collective_id=0, has_side_effects=True, vmem_limit_bytes=24 * 1024 * 1024
        ),
        name="gather_prompt",
    )(k, v)
    return out.reshape(2 * seq * rows, 2 * width)


def scatter_kernel(
    seq, mdl, stat_ref, pk_ref, pv_ref, coef_ref, dk_ref, dv_ref,
    stat_line, stat_group, from_pair, ready, arrived,
    line_send, line_recv, group_send, group_recv, pair_send, pair_recv, out_send, out_recv,
):
    me, core, lane = lax.axis_index("seq"), lax.axis_index("pair"), lax.axis_index("mdl")
    width = pk_ref.shape[2]
    line = [{"seq": lax.rem(me + off, seq)} for off in range(1, seq)]
    spot = lane * 2 + core
    group = []
    for off in range(1, 2 * mdl):
        other = lax.rem(spot + off, 2 * mdl)
        group.append({"mdl": other // 2, "pair": lax.rem(other, 2)})
    partner = {"pair": 1 - core}
    stat_line[me] = stat_ref[...]
    stat_group[spot] = stat_ref[...]
    enter(line + group)
    small, swaps, away = [], [], []
    for n, peer in enumerate(group):
        small.append(remote(stat_ref, stat_group.at[spot], group_send.at[n], group_recv.at[n], peer))
    for n, peer in enumerate(line):
        small.append(remote(stat_ref, stat_line.at[me], line_send.at[n], line_recv.at[n], peer))
    for half, ref in enumerate((pk_ref, pv_ref)):
        for n in range(seq):
            sems = (pair_send.at[half, n], pair_recv.at[half, n])
            swaps.append(remote(ref.at[n * 2 + 1 - core], from_pair.at[half, n], *sems, partner))
    for copy in small + swaps:
        copy.start()
    for copy in small:
        copy.wait()

    def gap(side):
        total = jnp.zeros((1, BLK), jnp.float32)
        for n in range(mdl):
            total += stat_group[n * 2 + side, 0:1, :]
        return jnp.sum(total, axis=1, keepdims=True) - stat_group[side, 1:2, :]

    sign = jnp.where(core == 0, 1.0, -1.0)
    margin = dpo_beta * sign * (gap(core) - gap(1 - core))
    own_count = jnp.zeros((1, BLK), jnp.float32)
    for n in range(seq):
        own_count += jnp.where(stat_line[n, 2:3, :] == stat_ref[2:3, :], 1.0, 0.0)
    weight = seq / (NDOM * own_count)
    coef = -sign * loss_scale * weight * dpo_beta * jax.nn.sigmoid(-margin)
    coef_ref[...] = jnp.broadcast_to(coef, coef_ref.shape)
    factor = jnp.concatenate([coef] * (width // BLK), axis=1)
    for copy in swaps:
        copy.wait()
    for half, ref in enumerate((pk_ref, pv_ref)):
        for n in range(seq):
            mine = ref[n * 2 + core].astype(jnp.float32) - from_pair[half, n].astype(jnp.float32)
            ready[n, :, half * width : (half + 1) * width] = (mine * factor).astype(ready.dtype)
    for n, peer in enumerate(line):
        copy = remote(ready.at[peer["seq"]], arrived.at[me], out_send.at[n], out_recv.at[n], peer)
        copy.start()
        away.append(copy)
    total = ready[me].astype(jnp.float32)
    for n, copy in enumerate(away):
        copy.wait()
        total += arrived[lax.rem(me + seq - n - 1, seq)].astype(jnp.float32)
    dk_ref[...] = total[:, :width]
    dv_ref[...] = total[:, width:]


def scatter(stat, pk, pv, rows):
    seq, mdl = lax.axis_size("seq"), lax.axis_size("mdl")
    width = pk.shape[1]
    f32, bf16, dma = jnp.float32, pk.dtype, pltpu.SemaphoreType.DMA
    vmem = pl.BlockSpec(memory_space=pltpu.VMEM)
    return pl.pallas_call(
        functools.partial(scatter_kernel, seq, mdl),
        out_shape=[
            jax.ShapeDtypeStruct((8, BLK), f32),
            jax.ShapeDtypeStruct((rows, width), f32),
            jax.ShapeDtypeStruct((rows, width), f32),
        ],
        in_specs=[vmem] * 3,
        out_specs=[vmem] * 3,
        scratch_shapes=[
            pltpu.VMEM((seq, 8, BLK), f32),
            pltpu.VMEM((2 * mdl, 8, BLK), f32),
            pltpu.VMEM((2, seq, rows, width), bf16),
            pltpu.VMEM((seq, rows, 2 * width), bf16),
            pltpu.VMEM((seq, rows, 2 * width), bf16),
            dma((seq,)), dma((seq,)), dma((2 * mdl,)), dma((2 * mdl,)),
            dma((2, seq)), dma((2, seq)), dma((seq,)), dma((seq,)),
        ],
        compiler_params=pltpu.CompilerParams(
            collective_id=1, has_side_effects=True, vmem_limit_bytes=24 * 1024 * 1024
        ),
        name="scatter_prompt_gradients",
    )(stat, pk.reshape(2 * seq, rows, width), pv.reshape(2 * seq, rows, width))


def per_device(
    resp_query, resp_key, response_value, readout, packed_prompt_key, packed_prompt_value,
    prompt_owner, pair_slot, domain_of, resp_blocks, ref_logprob,
):
    packed_kv = gather(packed_prompt_key, packed_prompt_value)
    dq, dk, dv, pk, pv, stat = attention(
        resp_query, readout, resp_key, response_value, packed_kv,
        prompt_owner[None, :], pair_slot, resp_blocks, domain_of, ref_logprob,
    )
    coef, key_prompt, value_prompt = scatter(stat, pk, pv, packed_prompt_key.shape[0])

    def scaled(array):
        return (array.astype(jnp.float32) * coef[0, 0]).astype(jnp.bfloat16)

    return scaled(dq), scaled(dk), scaled(dv), key_prompt, value_prompt


def solution(mesh):
    tokens = P(("grp", "seq", "pair"), "mdl")
    each = P(("grp", "seq", "pair"))
    in_specs = (tokens,) * 6 + (P("grp"), P(("grp", "seq")), P(("grp", "seq")), each, each)
    return jax.shard_map(per_device, mesh=mesh, in_specs=in_specs, out_specs=(tokens,) * 5, check_vma=False)
```

time: 143 us -> 88.2 us (0.62)
  waiting for transfers between devices: 49.3 us -> 0 us
  Pallas kernels: 38.2 us -> 70.5 us
  blocking collectives: 19 us -> 0 us
  between operations: 18.8 us -> 3.25 us
  other arithmetic: 10.4 us -> 7.72 us
    reduce_scatter x1 -> x0, waiting for transfers between devices: 40.1 us -> none  [per_device(): lax.psum_scatter(placed, ('seq', 'pair'), scatter_dimension=0, tiled=True)]
    pallas_call x1 -> x3, Pallas kernels: 38.2 us -> 70.5 us  [the longest x1 34.7 us: attention(): pl.pallas_call(functools.partial(attention_kernel, group, AT_ONCE), grid=...]
    psum x2 -> x0, blocking collectives: 19 us -> none  [the longest x1 13.5 us: per_device(): lax.psum(jnp.where(domain_slots == domain_of[0], 1.0, 0.0).astype(jnp.flo...]
    all_gather x1 -> x0, waiting for transfers between devices: 8.85 us -> none  [per_device(): gathered = lax.all_gather(packed, ('seq', 'pair'), axis=0, tiled=True)]
    unnamed x6 -> x12, local copies, waits for them, and re-layouts: 2.76 us -> 5.74 us
    slice x2 -> x1, local copies, waits for them, and re-layouts: 2.86 us -> 0.51 us  [scaled(): return (array.astype(jnp.float32) * coef[0, 0]).astype(jnp.bfloat16)]
    concatenate x1 -> x0, other arithmetic: 1.54 us -> none  [per_device(): packed = jnp.concatenate([packed_prompt_key, packed_prompt_value], axis=1)]
    convert_element_type x3 -> x2, other arithmetic: 7.62 us -> 7.72 us  [scaled(): return (array.astype(jnp.float32) * coef[0, 0]).astype(jnp.bfloat16)]
  transfers between devices with their start and end apart: 3 -> 0, of which waited for: 3 -> 0; matrix products, arithmetic and copies ran while one was open for 5% -> 0% of each run, Pallas kernels for 0% -> 0%
where the time goes in v2:
time: 88.2 us; the launch traced here: 87.8 us
  Pallas kernels  70.5 us (80%)
  other arithmetic  7.72 us (9%)
  local copies, waits for them, and re-layouts  6.25 us (7%)
  between operations  3.25 us (4%)
    pallas_call x1, Pallas kernels, attention(): pl.pallas_call(functools.partial(attention_kernel, group, AT_ONCE), grid=...  34.7 us
    pallas_call x1, Pallas kernels, scatter(): pl.pallas_call(functools.partial(scatter_kernel, seq, mdl), out_shape=[ja...  19.5 us
    pallas_call x1, Pallas kernels, gather(): pl.pallas_call(functools.partial(gather_kernel, seq), out_shape=jax.Shape...  16.3 us
    convert_element_type x2, other arithmetic, scaled(): return (array.astype(jnp.float32) * coef[0, 0]).astype(jnp.bfloat16)  7.72 us
    unnamed x12, local copies, waits for them, and re-layouts  5.74 us

profile of v2, /device:TPU:0, one launch (start us, length us, event | category | flops | bytes accessed | tf_op | source)
XLA Modules:
  0.0 87.8 jit_solution(7672558182749663451)
XLA Ops:
  3.2 0.0 copy-start
  3.2 0.8 copy-done
  4.1 0.0 copy-start.1
  4.1 0.8 copy-done.1
  4.9 16.3 %gather_prompt.1 = bf16[8,64,1024]{2,1,0:T(8,128)(2,1)S(1)} custom-call(bf16[64,512]{1,0:T(8,128)(2,1)S(1)} %copy-done, bf16[64,512]{1,0:T(8,128)(2,1)S(1)} %copy-done.1), custom_call_target="tpu_custom_call" | custom-call | tf_op jit(solution)/shard_map/gather_prompt/pallas_call | solution.py:205
  21.2 0.0 copy-start.2
  21.3 1.0 %copy-done.2 = bf16[512,512]{1,0:T(8,128)(2,1)S(1)} copy-done((bf16[512,512]{1,0:T(8,128)(2,1)S(1)}, bf16[512,512]{1,0:T(8,128)(2,1)}, u32[]{:S(2)}) %copy-start.2) | copy-done | bytes 524312
  22.3 0.0 copy-start.3
  22.3 1.0 %copy-done.3 = bf16[512,512]{1,0:T(8,128)(2,1)S(1)} copy-done((bf16[512,512]{1,0:T(8,128)(2,1)S(1)}, bf16[512,512]{1,0:T(8,128)(2,1)}, u32[]{:S(2)}) %copy-start.3) | copy-done | bytes 524312
  23.3 0.0 copy-start.4
  23.3 0.7 copy-done.4
  24.0 34.7 %attention_gradients.1 = (bf16[512,4096]{1,0:T(8,128)(2,1)}, bf16[512,512]{1,0:T(8,128)(2,1)S(1)}, bf16[512,512]{1,0:T(8,128)(2,1)S(1)}, bf16[512,512]{1,0:T(8,1...) custom-call(s32[1]{0:T(128)S(6)} %copy.20.blocks_ref, s32[1]{0:T(128)S(6)} %copy.18.slot_ref, ...), custom_call_target="tpu_custom_call" | custom-call | flops 12000000000 | bytes 16777216 | tf_op jit(solution)/shard_map/attention_gradients/pallas_call | solution.py:131
  58.7 19.5 %scatter_prompt_gradients.1 = (f32[8,128]{1,0:T(8,128)S(1)}, f32[64,512]{1,0:T(8,128)S(1)}, f32[64,512]{1,0:T(8,128)S(1)}) custom-call(f32[8,128]{1,0:T(8,128)S(1)} %get-tuple-element.15.stat_ref, bf16[8,64,512]{2,1,0:T(8,128)(2,1)S(1)} %bitcast.7, bf16[8,64,512]{2,1,0:T(8,128)(2,1)S(1)} %bitcast.8), custom_call_target="tpu_custom_call" | custom-call | tf_op jit(solution)/shard_map/scatter_prompt_gradients/pallas_call | solution.py:288
  78.2 0.5 slice.2
  78.7 5.9 %multiply_convert_fusion = bf16[512,4096]{1,0:T(8,128)(2,1)} fusion(bf16[512,4096]{1,0:T(8,128)(2,1)} %get-tuple-element.14, f32[]{:T(128)} %bitcast.4), kind=kLoop, calls=%fused_computation | loop fusion | flops 6291456 | bytes 8388612 | tf_op jit(solution)/shard_map/convert_element_type | solution.py:325
  84.6 1.8 %multiply_convert_fusion.1 = (bf16[512,512]{1,0:T(8,128)(2,1)}, bf16[512,512]{1,0:T(8,128)(2,1)}) fusion(bf16[512,512]{1,0:T(8,128)(2,1)S(1)} %get-tuple-element.20, f32[]{:T(128)} %bitcast.4, bf16[512,512]{1,0:T(8,128)(2,1)S(1)} %get-tuple-element.19), kind=kLoop, calls=%fused_computation.1 | loop fusion | flops 1572864 | bytes 2097156 | tf_op jit(solution)/shard_map/convert_element_type | solution.py:325
  86.5 0.7 copy.22
  87.1 0.7 copy.23
Async XLA Ops:
  3.2 0.8 copy-start
  4.1 0.8 copy-start.1
  21.2 1.0 %copy-start.2 = (bf16[512,512]{1,0:T(8,128)(2,1)S(1)}, bf16[512,512]{1,0:T(8,128)(2,1)}, u32[]{:S(2)}) copy-start(bf16[512,512]{1,0:T(8,128)(2,1)} %k_ref.3) | copy-start | bytes 1572868
  22.3 1.0 %copy-start.3 = (bf16[512,512]{1,0:T(8,128)(2,1)S(1)}, bf16[512,512]{1,0:T(8,128)(2,1)}, u32[]{:S(2)}) copy-start(bf16[512,512]{1,0:T(8,128)(2,1)} %v_ref.3) | copy-start | bytes 1572868
  23.3 0.7 copy-start.4

commit v3 on v2

--- a/solution.py
+++ b/solution.py
@@ -14,6 +14,7 @@
 NDOM = 8
 WINDOW = 4 * PROMPT_DEV
 NEG = -1e30
+VMEM_BYTES = 60 * 2**20
 AT_ONCE = 2
 
 dpo_beta = 0.5
@@ -152,7 +153,7 @@
             pltpu.VMEM((keys, HEAD_SIZE), f32),
             pltpu.VMEM((keys, HEAD_SIZE), f32),
         ],
-        compiler_params=pltpu.CompilerParams(vmem_limit_bytes=48 * 1024 * 1024),
+        compiler_params=pltpu.CompilerParams(vmem_limit_bytes=VMEM_BYTES),
         cost_estimate=pl.CostEstimate(flops=12 * 10**9, bytes_accessed=16 * 2**20, transcendentals=10**7),
         name="attention_gradients",
     )(blocks, slot, domain, ref, owner, q, r, k, v, packed_kv, packed_kv)
@@ -209,7 +210,7 @@
         out_specs=pl.BlockSpec(memory_space=pltpu.VMEM),
         scratch_shapes=[dma((seq,)), dma((seq,)), dma((seq,)), dma((seq,))],
         compiler_params=pltpu.CompilerParams(
-            collective_id=0, has_side_effects=True, vmem_limit_bytes=24 * 1024 * 1024
+            collective_id=0, has_side_effects=True, vmem_limit_bytes=VMEM_BYTES
         ),
         name="gather_prompt",
     )(k, v)
@@ -217,8 +218,8 @@
 
 
 def scatter_kernel(
-    seq, mdl, stat_ref, pk_ref, pv_ref, coef_ref, dk_ref, dv_ref,
-    stat_line, stat_group, from_pair, ready, arrived,
+    seq, mdl, stat_ref, pk_ref, pv_ref, gq_ref, gk_ref, gv_ref, dk_ref, dv_ref, oq_ref, ok_ref, ov_ref,
+    held, load_sem, store_sem, stat_line, stat_group, from_pair, ready, arrived,
     line_send, line_recv, group_send, group_recv, pair_send, pair_recv, out_send, out_recv,
 ):
     me, core, lane = lax.axis_index("seq"), lax.axis_index("pair"), lax.axis_index("mdl")
@@ -230,6 +231,11 @@
         other = lax.rem(spot + off, 2 * mdl)
         group.append({"mdl": other // 2, "pair": lax.rem(other, 2)})
     partner = {"pair": 1 - core}
+    parts = [pl.ds(start, BLK) for start in range(0, held.shape[0], BLK)]
+    loads = [pltpu.make_async_copy(gq_ref.at[p], held.at[p], load_sem.at[n]) for n, p in enumerate(parts)]
+    stores = [pltpu.make_async_copy(held.at[p], oq_ref.at[p], store_sem.at[n]) for n, p in enumerate(parts)]
+    for copy in loads:
+        copy.start()
     stat_line[me] = stat_ref[...]
     stat_group[spot] = stat_ref[...]
     enter(line + group)
@@ -260,7 +266,6 @@
         own_count += jnp.where(stat_line[n, 2:3, :] == stat_ref[2:3, :], 1.0, 0.0)
     weight = seq / (NDOM * own_count)
     coef = -sign * loss_scale * weight * dpo_beta * jax.nn.sigmoid(-margin)
-    coef_ref[...] = jnp.broadcast_to(coef, coef_ref.shape)
     factor = jnp.concatenate([coef] * (width // BLK), axis=1)
     for copy in swaps:
         copy.wait()
@@ -272,29 +277,43 @@
         copy = remote(ready.at[peer["seq"]], arrived.at[me], out_send.at[n], out_recv.at[n], peer)
         copy.start()
         away.append(copy)
+    wide = jnp.concatenate([coef] * (held.shape[1] // BLK), axis=1)
+    for n, p in enumerate(parts):
+        loads[n].wait()
+        held[p] = (held[p].astype(jnp.float32) * wide).astype(held.dtype)
+        stores[n].start()
+    ok_ref[...] = (gk_ref[...].astype(jnp.float32) * factor).astype(ok_ref.dtype)
+    ov_ref[...] = (gv_ref[...].astype(jnp.float32) * factor).astype(ov_ref.dtype)
     total = ready[me].astype(jnp.float32)
     for n, copy in enumerate(away):
         copy.wait()
         total += arrived[lax.rem(me + seq - n - 1, seq)].astype(jnp.float32)
     dk_ref[...] = total[:, :width]
     dv_ref[...] = total[:, width:]
-
-
-def scatter(stat, pk, pv, rows):
+    for copy in stores:
+        copy.wait()
+
+
+def scatter(stat, pk, pv, dq, dk, dv, rows):
     seq, mdl = lax.axis_size("seq"), lax.axis_size("mdl")
     width = pk.shape[1]
     f32, bf16, dma = jnp.float32, pk.dtype, pltpu.SemaphoreType.DMA
     vmem = pl.BlockSpec(memory_space=pltpu.VMEM)
+    whole = pl.BlockSpec(memory_space=pl.ANY)
     return pl.pallas_call(
         functools.partial(scatter_kernel, seq, mdl),
         out_shape=[
-            jax.ShapeDtypeStruct((8, BLK), f32),
             jax.ShapeDtypeStruct((rows, width), f32),
             jax.ShapeDtypeStruct((rows, width), f32),
+            jax.ShapeDtypeStruct(dq.shape, dq.dtype),
+            jax.ShapeDtypeStruct(dk.shape, dk.dtype),
+            jax.ShapeDtypeStruct(dv.shape, dv.dtype),
         ],
-        in_specs=[vmem] * 3,
-        out_specs=[vmem] * 3,
+        in_specs=[vmem] * 3 + [whole, vmem, vmem],
+        out_specs=[vmem] * 2 + [whole, vmem, vmem],
         scratch_shapes=[
+            pltpu.VMEM(dq.shape, dq.dtype),
+            dma((dq.shape[0] // BLK,)), dma((dq.shape[0] // BLK,)),
             pltpu.VMEM((seq, 8, BLK), f32),
             pltpu.VMEM((2 * mdl, 8, BLK), f32),
             pltpu.VMEM((2, seq, rows, width), bf16),
@@ -304,10 +323,10 @@
             dma((2, seq)), dma((2, seq)), dma((seq,)), dma((seq,)),
         ],
         compiler_params=pltpu.CompilerParams(
-            collective_id=1, has_side_effects=True, vmem_limit_bytes=24 * 1024 * 1024
+            collective_id=1, has_side_effects=True, vmem_limit_bytes=VMEM_BYTES
         ),
         name="scatter_prompt_gradients",
-    )(stat, pk.reshape(2 * seq, rows, width), pv.reshape(2 * seq, rows, width))
+    )(stat, pk.reshape(2 * seq, rows, width), pv.reshape(2 * seq, rows, width), dq, dk, dv)
 
 
 def per_device(
@@ -319,12 +338,8 @@
         resp_query, readout, resp_key, response_value, packed_kv,
         prompt_owner[None, :], pair_slot, resp_blocks, domain_of, ref_logprob,
     )
-    coef, key_prompt, value_prompt = scatter(stat, pk, pv, packed_prompt_key.shape[0])
-
-    def scaled(array):
-        return (array.astype(jnp.float32) * coef[0, 0]).astype(jnp.bfloat16)
-
-    return scaled(dq), scaled(dk), scaled(dv), key_prompt, value_prompt
+    key_prompt, value_prompt, dq, dk, dv = scatter(stat, pk, pv, dq, dk, dv, packed_prompt_key.shape[0])
+    return dq, dk, dv, key_prompt, value_prompt
 
 
 def solution(mesh):

time: 88.2 us -> 87 us (0.986)
  other arithmetic: 7.72 us -> 0 us
  Pallas kernels: 70.5 us -> 75.8 us
  local copies, waits for them, and re-layouts: 6.25 us -> 7.71 us
    convert_element_type x2 -> x0, other arithmetic: 7.72 us -> none  [scaled(): return (array.astype(jnp.float32) * coef[0, 0]).astype(jnp.bfloat16)]
    pallas_call x1, Pallas kernels: 19.5 us -> 22.2 us  [scatter(): pl.pallas_call(functools.partial(scatter_kernel, seq, mdl), out_shape=[ja...]
    unnamed x12 -> x13, local copies, waits for them, and re-layouts: 5.74 us -> 7.71 us
    pallas_call x1, Pallas kernels: 16.3 us -> 18.2 us  [gather(): pl.pallas_call(functools.partial(gather_kernel, seq), out_shape=jax.Shape...]
where the time goes in v3:
time: 87 us; the launch traced here: 86.8 us
  Pallas kernels  75.8 us (87%)
  local copies, waits for them, and re-layouts  7.71 us (9%)
  between operations  3.27 us (4%)
    pallas_call x1, Pallas kernels, attention(): pl.pallas_call(functools.partial(attention_kernel, group, AT_ONCE), grid=...  35.4 us
    pallas_call x1, Pallas kernels, scatter(): pl.pallas_call(functools.partial(scatter_kernel, seq, mdl), out_shape=[ja...  22.2 us
    pallas_call x1, Pallas kernels, gather(): pl.pallas_call(functools.partial(gather_kernel, seq), out_shape=jax.Shape...  18.2 us
    unnamed x13, local copies, waits for them, and re-layouts  7.71 us

profile of v3, /device:TPU:0, one launch (start us, length us, event | category | flops | bytes accessed | tf_op | source)
XLA Modules:
  0.0 86.8 jit_solution(13412689962046584749)
XLA Ops:
  3.2 18.2 %gather_prompt.1 = bf16[8,64,1024]{2,1,0:T(8,128)(2,1)} custom-call(bf16[64,512]{1,0:T(8,128)(2,1)} %k_ref.2, bf16[64,512]{1,0:T(8,128)(2,1)} %v_ref.2), custom_call_target="tpu_custom_call" | custom-call | tf_op jit(solution)/shard_map/gather_prompt/pallas_call | solution.py:206
  21.4 35.4 %attention_gradients.1 = (bf16[512,4096]{1,0:T(8,128)(2,1)}, bf16[512,512]{1,0:T(8,128)(2,1)}, bf16[512,512]{1,0:T(8,128)(2,1)}, bf16[512,512]{1,0:T(8,128)(2,1)...) custom-call(s32[1]{0:T(128)S(6)} %copy.23.blocks_ref, s32[1]{0:T(128)S(6)} %copy.21.slot_ref, s32[1]{0:T(128)S(6)} %copy.22.domain_ref, ...), custom_call_target="tpu_custom_call" | custom-call | flops 12000000000 | bytes 16777216 | tf_op jit(solution)/shard_map/attention_gradients/pallas_call | solution.py:132
  56.8 22.2 %scatter_prompt_gradients.1 = (f32[64,512]{1,0:T(8,128)}, f32[64,512]{1,0:T(8,128)}, bf16[512,4096]{1,0:T(8,128)(2,1)}, bf16[512,512]{1,0:T(8,128)(2,1)}, bf16[512,512]{1,0:T(8,128)(2,1)}) custom-call(f32[8,128]{1,0:T(8,128)} %get-tuple-element.16.stat_ref, bf16[8,64,512]{2,1,0:T(8,128)(2,1)} %bitcast.6, bf16[8,64,512]{2,1,0:T(8,128)(2,1)} %bitcast.7, ...), custom_call_target="tpu_custom_call" | custom-call | tf_op jit(solution)/shard_map/scatter_prompt_gradients/pallas_call | solution.py:303
  79.1 0.0 copy-start.1
  79.1 0.0 copy-start
  79.1 0.0 copy-start.3
  79.1 0.0 copy-start.2
  79.1 4.8 %copy.25 = bf16[512,4096]{1,0:T(8,128)(2,1)} copy(bf16[512,4096]{1,0:T(8,128)(2,1)} %get-tuple-element.32) | data formatting | bytes 8388608
  83.9 0.0 copy-done.1
  83.9 0.8 copy.26
  84.7 0.0 copy-done
  84.7 0.8 copy.27
  85.5 0.0 copy-done.3
  85.5 0.7 copy.28
  86.2 0.0 copy-done.2
  86.2 0.7 copy.29
Async XLA Ops:
  79.1 4.8 %copy-start.1 = (bf16[512,512]{1,0:T(8,128)(2,1)S(1)}, bf16[512,512]{1,0:T(8,128)(2,1)}, u32[]{:S(2)}) copy-start(bf16[512,512]{1,0:T(8,128)(2,1)} %get-tuple-element.33) | copy-start | bytes 1572868
  79.1 5.6 %copy-start = (bf16[512,512]{1,0:T(8,128)(2,1)S(1)}, bf16[512,512]{1,0:T(8,128)(2,1)}, u32[]{:S(2)}) copy-start(bf16[512,512]{1,0:T(8,128)(2,1)} %get-tuple-element.34) | copy-start | bytes 1572868
  79.1 6.4 %copy-start.3 = (f32[64,512]{1,0:T(8,128)S(1)}, f32[64,512]{1,0:T(8,128)}, u32[]{:S(2)}) copy-start(f32[64,512]{1,0:T(8,128)} %get-tuple-element.35) | copy-start | bytes 393220
  79.1 7.1 %copy-start.2 = (f32[64,512]{1,0:T(8,128)S(1)}, f32[64,512]{1,0:T(8,128)}, u32[]{:S(2)}) copy-start(f32[64,512]{1,0:T(8,128)} %get-tuple-element.36) | copy-start | bytes 393220
